TPU v7x, 32 devices: a whole 2x2x4 slice. The times are simulated.
32 devices in a mesh: tower: 2 (over core), rows: 16 (over z, y, x).
Axes of the slice: x: 2, y: 2, z: 4, core: 2. Of those that a mesh axis runs over, the one named last changes fastest.
Arguments:
- tokens: bfloat16 [2, 32, 512, 512], P('tower', 'rows'), may hold values from -9 to 9
- segment_ids: int32 [2, 32, 512], P('tower', 'rows'), may hold values from 0 to 8, never falling along the last dimension, each value on 1 to 128 neighbouring positions
- positives: int32 [256], P('rows'), may hold values from 0 to 255, each once
- attention_gain: float32 [512], replicated, may hold values from 0.5 to 1.5
- query_weight: bfloat16 [512, 512], replicated, may hold values from -0.0625 to 0.0625
- key_weight: bfloat16 [512, 512], replicated, may hold values from -0.25 to 0.25
- value_weight: bfloat16 [512, 512], replicated, may hold values from -0.25 to 0.25
- output_weight: bfloat16 [512, 512], replicated, may hold values from -1 to 1
- position_table: float32 [32, 8], replicated, may hold values from -3 to 3
- feedforward_gain: float32 [512], replicated, may hold values from 0.5 to 1.5
- inner_weight: bfloat16 [512, 2048], replicated, may hold values from -0.25 to 0.25
- outer_weight: bfloat16 [2048, 512], replicated, may hold values from -0.1875 to 0.1875
Outputs:
- layer_output: bfloat16 [2, 32, 512, 512], P('tower', 'rows')
- token_grad: bfloat16 [2, 32, 512, 512], P('tower', 'rows')
- attention_gain_grad: float32 [512], replicated
- query_grad: float32 [512, 512], replicated
- key_grad: float32 [512, 512], replicated
- value_grad: float32 [512, 512], replicated
- output_grad: float32 [512, 512], replicated
- position_grad: float32 [32, 8], replicated
- feedforward_gain_grad: float32 [512], replicated
- inner_grad: float32 [512, 2048], replicated
- outer_grad: float32 [2048, 512], replicated
- contrastive_loss: float32 [], replicated
- root_mean_squares: float32 [3], replicated
Inputs may be any that keep to these rules, and one draw needn't show every extreme that they name: `segment_ids`: within each row of 512 tokens the numbers never fall; 0 to 7 are the row's items and 8 marks the padding at its end; every number, padding included, covers 1 to 128 tokens. positives[m] is the document item paired with query item m; every document item occurs once.
All inputs are finite; a program needn't handle non-finite values.
Results may differ from a plain program's by a relative error of at most 0.028.
The roundings to bfloat16 on the way count: a program that leaves them out, or rounds other values in their place, can miss the bound.
Values sent between devices are 32-bit elements; how exact they have to be, the bound alone decides.
A program may use at most 320 MiB of HBM per device.

v0:
```python
import math
import jax
import jax.numpy as jnp
import numpy as np
from jax import lax
from jax.sharding import PartitionSpec as P

MAX_DIST = 128
ITEMS_ROW = 8
EPSILON = 1e-06
SOFTMAX_TEMP = 0.01
LOSS_SCALE = 65536.0
MATMUL_PRECISION = lax.Precision.HIGHEST


def from_partner(value, axis, apart):
    mask = 2**apart
    pairs = [(source, source ^ mask) for source in range(lax.axis_size(axis))]
    return lax.ppermute(value, axis, pairs)


def bucket_table(length, bucket_count, far_limit):
    half_count = bucket_count // 2
    exact_count = half_count // 2
    entries = []
    for offset in range(1 - length, length):
        distance = abs(offset)
        if distance < exact_count:
            within = distance
        else:
            within = exact_count + int(
                math.log(distance / exact_count)
                / math.log(far_limit / exact_count)
                * (half_count - exact_count)
            )
            within = min(within, half_count - 1)
        entries.append(within + (half_count if offset > 0 else 0))
    by_offset = np.array(entries, dtype=np.int32)
    index_grid = np.arange(length)[None, :] - np.arange(length)[:, None] + length - 1
    return (by_offset, by_offset[index_grid])


def contract_rows(left_side, right_side):
    return lax.dot_general(
        left_side, right_side, (((0,), (0,)), ((), ())), preferred_element_type=jnp.float32
    )


def times_transpose(left_side, right_side):
    return lax.dot_general(
        left_side, right_side, (((1,), (1,)), ((), ())), preferred_element_type=jnp.float32
    )


def norm_scale(values):
    return lax.rsqrt(jnp.mean(values * values, axis=1, keepdims=True) + EPSILON)


def norm_back(grad_normed, values, scale, gain):
    gained = grad_normed * gain
    return scale * (
        gained - values * scale * scale * jnp.mean(gained * values, axis=1, keepdims=True)
    )


def row_scores(query_part, key_part, segment_row, position_bias, head_count):
    length = query_part.shape[0]
    query_heads = query_part.reshape(length, head_count, -1)
    key_heads = key_part.reshape(length, head_count, -1)
    scores = (
        jnp.einsum("qhd,khd->hqk", query_heads, key_heads, preferred_element_type=jnp.float32)
        + position_bias
    )
    same_item = segment_row[:, None] == segment_row[None, :]
    return jnp.where(same_item[None], scores, -1e30)


def diagonal_sums(square):
    head_count = square.shape[0]
    length = square.shape[1]
    flipped = square[:, :, ::-1]
    padded = jnp.pad(flipped, ((0, 0), (0, 0), (0, length)))
    sheared = padded.reshape(head_count, 2 * length * length)[:, : length * (2 * length - 1)]
    sheared = sheared.reshape(head_count, length, 2 * length - 1)
    return jnp.sum(sheared, axis=1)[:, ::-1]


def shards(
    tokens,
    segment_ids,
    positives,
    attention_gain,
    query_weight,
    key_weight,
    value_weight,
    output_weight,
    position_table,
    feedforward_gain,
    inner_weight,
    outer_weight,
):
    row_count = tokens.shape[1]
    length = tokens.shape[2]
    model_width = tokens.shape[3]
    head_count = position_table.shape[1]
    inner_width = query_weight.shape[1]
    head_size = inner_width // head_count
    token_count = row_count * length
    by_offset, bucket_index = bucket_table(length, position_table.shape[0], MAX_DIST)
    position_bias = jnp.take(position_table.T, jnp.asarray(bucket_index), axis=1)
    inputs = tokens.reshape(token_count, model_width).astype(jnp.float32)
    segments = segment_ids.reshape(row_count, length)
    scale_one = norm_scale(inputs)
    normed_one = (inputs * scale_one * attention_gain).astype(jnp.bfloat16)
    query_rows = jnp.dot(normed_one, query_weight, preferred_element_type=jnp.float32).astype(
        jnp.bfloat16
    )
    key_rows = jnp.dot(normed_one, key_weight, preferred_element_type=jnp.float32).astype(
        jnp.bfloat16
    )
    value_rows = jnp.dot(normed_one, value_weight, preferred_element_type=jnp.float32).astype(
        jnp.bfloat16
    )
    query_blocks = query_rows.reshape(row_count, length, inner_width)
    key_blocks = key_rows.reshape(row_count, length, inner_width)
    value_blocks = value_rows.reshape(row_count, length, inner_width)

    def attend(packed):
        query_part, key_part, value_part, segment_row = packed
        scores = row_scores(query_part, key_part, segment_row, position_bias, head_count)
        highest = jnp.max(scores, axis=2, keepdims=True)
        exp_scores = jnp.exp(scores - highest)
        exp_total = jnp.sum(exp_scores, axis=2, keepdims=True)
        attention_probs = (exp_scores / exp_total).astype(jnp.bfloat16)
        value_heads = value_part.reshape(length, head_count, head_size)
        mixed_heads = jnp.einsum(
            "hqk,khd->qhd", attention_probs, value_heads, preferred_element_type=jnp.float32
        )
        return (
            mixed_heads.reshape(length, inner_width).astype(jnp.bfloat16),
            (highest + jnp.log(exp_total))[:, :, 0],
        )

    mixed_blocks, log_totals = lax.map(attend, (query_blocks, key_blocks, value_blocks, segments))
    mixed_rows = mixed_blocks.reshape(token_count, inner_width)
    branch_one = jnp.dot(mixed_rows, output_weight, preferred_element_type=jnp.float32)
    middle = inputs + branch_one
    scale_two = norm_scale(middle)
    normed_two = (middle * scale_two * feedforward_gain).astype(jnp.bfloat16)
    hidden = jax.nn.relu(
        jnp.dot(normed_two, inner_weight, preferred_element_type=jnp.float32)
    ).astype(jnp.bfloat16)
    branch_two = jnp.dot(hidden, outer_weight, preferred_element_type=jnp.float32)
    result = middle + branch_two
    valid_mask = (segments < ITEMS_ROW).astype(jnp.float32).reshape(token_count, 1)
    stat_terms = jnp.stack(
        [
            jnp.sum(valid_mask * result * result),
            jnp.sum(valid_mask * branch_one * branch_one),
            jnp.sum(valid_mask * branch_two * branch_two),
            jnp.sum(valid_mask),
        ]
    )
    stat_totals = lax.psum(stat_terms, ("tower", "rows"))
    member = (segments[:, None, :] == jnp.arange(ITEMS_ROW)[None, :, None]).astype(jnp.float32)
    item_sizes = jnp.sum(member, axis=2, keepdims=True)
    result_blocks = result.reshape(row_count, length, model_width)
    pooled = (
        jnp.einsum("ris,rsd->rid", member, result_blocks, precision=MATMUL_PRECISION) / item_sizes
    )
    items_here = row_count * ITEMS_ROW
    pooled = pooled.reshape(items_here, model_width)
    inverse_norm = lax.rsqrt(jnp.sum(pooled * pooled, axis=1, keepdims=True) + EPSILON)
    embedded_tokens = pooled * inverse_norm
    tower_index = lax.axis_index("tower")
    is_query = tower_index == 0
    partner = from_partner(embedded_tokens, "tower", 0)
    query_vectors = jnp.where(is_query, embedded_tokens, partner)
    document_vectors = jnp.where(is_query, partner, embedded_tokens)
    gathered_documents = lax.all_gather(document_vectors, "rows", axis=0, tiled=True)
    item_total = gathered_documents.shape[0]
    half_items = items_here // 2
    my_queries = lax.dynamic_slice_in_dim(query_vectors, tower_index * half_items, half_items, 0)
    my_targets = lax.dynamic_slice_in_dim(positives, tower_index * half_items, half_items, 0)
    similarity_scores = (
        lax.dot_general(
            my_queries,
            gathered_documents,
            (((1,), (1,)), ((), ())),
            precision=MATMUL_PRECISION,
            preferred_element_type=jnp.float32,
        )
        / SOFTMAX_TEMP
    )
    highest = jnp.max(similarity_scores, axis=1, keepdims=True)
    exp_logits = jnp.exp(similarity_scores - highest)
    exp_total = jnp.sum(exp_logits, axis=1, keepdims=True)
    log_total = highest[:, 0] + jnp.log(exp_total[:, 0])
    is_target = jnp.arange(item_total)[None, :] == my_targets[:, None]
    target = jnp.sum(jnp.where(is_target, similarity_scores, 0.0), axis=1)
    loss_part = jnp.sum(log_total - target)
    similarity_gradient = (exp_logits / exp_total - is_target.astype(jnp.float32)) * (
        LOSS_SCALE / item_total
    )
    local_gradient = (
        jnp.dot(similarity_gradient, gathered_documents, precision=MATMUL_PRECISION) / SOFTMAX_TEMP
    )
    grad_documents = lax.psum_scatter(
        lax.dot_general(
            similarity_gradient,
            my_queries,
            (((0,), (0,)), ((), ())),
            precision=MATMUL_PRECISION,
            preferred_element_type=jnp.float32,
        )
        / SOFTMAX_TEMP,
        "rows",
        scatter_dimension=0,
        tiled=True,
    )
    partner_mine, partner_documents = from_partner((local_gradient, grad_documents), "tower", 0)
    query_side = jnp.where(
        is_query,
        jnp.concatenate([local_gradient, partner_mine], 0),
        jnp.concatenate([partner_mine, local_gradient], 0),
    )
    own_grad = jnp.where(is_query, query_side, grad_documents + partner_documents)
    inner_along = jnp.sum(own_grad * embedded_tokens, axis=1, keepdims=True)
    grad_pooled = inverse_norm * (own_grad - embedded_tokens * inner_along)
    per_token = grad_pooled.reshape(row_count, ITEMS_ROW, model_width) / item_sizes
    grad_result = jnp.einsum("ris,rid->rsd", member, per_token, precision=MATMUL_PRECISION).reshape(
        token_count, model_width
    )
    grad_branch_two = grad_result.astype(jnp.bfloat16)
    outer_grad = contract_rows(hidden, grad_branch_two)
    grad_hidden = times_transpose(grad_branch_two, outer_weight)
    grad_pre = jnp.where(hidden > 0, grad_hidden, 0.0).astype(jnp.bfloat16)
    inner_grad = contract_rows(normed_two, grad_pre)
    grad_normed_two = times_transpose(grad_pre, inner_weight)
    feedforward_gain_grad = jnp.sum(grad_normed_two * middle * scale_two, axis=0)
    grad_middle = grad_result + norm_back(grad_normed_two, middle, scale_two, feedforward_gain)
    grad_branch_one = grad_middle.astype(jnp.bfloat16)
    output_grad = contract_rows(mixed_rows, grad_branch_one)
    grad_mixed = times_transpose(grad_branch_one, output_weight).astype(jnp.bfloat16)
    grad_mixed_blocks = grad_mixed.reshape(row_count, length, inner_width)

    def attend_back(running, packed):
        query_part, key_part, value_part, segment_row, row_log_total, grad_part = packed
        scores = row_scores(query_part, key_part, segment_row, position_bias, head_count)
        attention_probs = jnp.exp(scores - row_log_total[:, :, None])
        query_heads = query_part.reshape(length, head_count, head_size)
        key_heads = key_part.reshape(length, head_count, head_size)
        value_heads = value_part.reshape(length, head_count, head_size)
        grad_heads = grad_part.reshape(length, head_count, head_size)
        grad_value = jnp.einsum(
            "hqk,qhd->khd",
            attention_probs.astype(jnp.bfloat16),
            grad_heads,
            preferred_element_type=jnp.float32,
        )
        grad_probs = jnp.einsum(
            "qhd,khd->hqk", grad_heads, value_heads, preferred_element_type=jnp.float32
        )
        row_dot = jnp.sum(attention_probs * grad_probs, axis=2, keepdims=True)
        grad_scores = (attention_probs * (grad_probs - row_dot)).astype(jnp.bfloat16)
        grad_query = jnp.einsum(
            "hqk,khd->qhd", grad_scores, key_heads, preferred_element_type=jnp.float32
        )
        grad_key = jnp.einsum(
            "hqk,qhd->khd", grad_scores, query_heads, preferred_element_type=jnp.float32
        )
        outputs = (
            grad_query.reshape(length, inner_width).astype(jnp.bfloat16),
            grad_key.reshape(length, inner_width).astype(jnp.bfloat16),
            grad_value.reshape(length, inner_width).astype(jnp.bfloat16),
        )
        return (running + grad_scores.astype(jnp.float32), outputs)

    score_sum, grad_rows = lax.scan(
        attend_back,
        jnp.zeros((head_count, length, length), jnp.float32),
        (query_blocks, key_blocks, value_blocks, segments, log_totals, grad_mixed_blocks),
    )
    grad_queries = grad_rows[0].reshape(token_count, inner_width)
    grad_keys = grad_rows[1].reshape(token_count, inner_width)
    grad_values = grad_rows[2].reshape(token_count, inner_width)
    query_grad = contract_rows(normed_one, grad_queries)
    key_grad = contract_rows(normed_one, grad_keys)
    value_grad = contract_rows(normed_one, grad_values)
    grad_normed_one = (
        times_transpose(grad_queries, query_weight)
        + times_transpose(grad_keys, key_weight)
        + times_transpose(grad_values, value_weight)
    )
    attention_gain_grad = jnp.sum(grad_normed_one * inputs * scale_one, axis=0)
    token_grad = grad_middle + norm_back(grad_normed_one, inputs, scale_one, attention_gain)
    offset_onehot = jnp.asarray(
        (by_offset[:, None] == np.arange(position_table.shape[0])[None, :]).astype(np.float32)
    )
    position_grad = jnp.dot(diagonal_sums(score_sum), offset_onehot, precision=MATMUL_PRECISION).T
    closing_terms = loss_part[None]
    summed = lax.psum(
        (
            attention_gain_grad,
            query_grad,
            key_grad,
            value_grad,
            output_grad,
            position_grad,
            feedforward_gain_grad,
            inner_grad,
            outer_grad,
            closing_terms,
        ),
        ("tower", "rows"),
    )
    (
        attention_gain_grad,
        query_grad,
        key_grad,
        value_grad,
        output_grad,
        position_grad,
        feedforward_gain_grad,
        inner_grad,
        outer_grad,
        closing_totals,
    ) = summed
    contrastive_loss = closing_totals[0] / item_total
    root_mean_squares = jnp.sqrt(stat_totals[:3] / (stat_totals[3] * model_width))
    block_shape = (1, row_count, length, model_width)
    return (
        result.reshape(block_shape).astype(jnp.bfloat16),
        token_grad.reshape(block_shape).astype(jnp.bfloat16),
        attention_gain_grad,
        query_grad,
        key_grad,
        value_grad,
        output_grad,
        position_grad,
        feedforward_gain_grad,
        inner_grad,
        outer_grad,
        contrastive_loss,
        root_mean_squares,
    )


def solution(mesh):
    return jax.shard_map(
        shards,
        mesh=mesh,
        in_specs=(
            P("tower", "rows", None, None),
            P("tower", "rows", None),
            P("rows"),
            P(),
            P(),
            P(),
            P(),
            P(),
            P(),
            P(),
            P(),
            P(),
        ),
        out_specs=(
            P("tower", "rows", None, None),
            P("tower", "rows", None, None),
            P(),
            P(),
            P(),
            P(),
            P(),
            P(),
            P(),
            P(),
            P(),
            P(),
            P(),
        ),
        check_vma=False,
    )
```

profile of v0, /device:TPU:0, one launch (start us, length us, event | category | flops | bytes accessed | tf_op | source)
XLA Modules:
  0.0 1486.5 jit_solution(8252469070416313084)
XLA Ops:
  26.5 865.7 %gather_fusion = f32[262144,8]{1,0:T(8,128)} fusion(f32[8,32]{0,1:T(8,128)S(1)} %bitcast.203, s32[262144]{0:T(1024)S(1)} %broadcast_clamp_fusion), kind=kCustom, calls=%fused_computation | custom fusion | bytes 17825792 | tf_op jit(solution)/shard_map/jit(_take)/gather | solution.py:110
  892.2 70.9 %copy.45 = f32[512,512,8]{0,1,2:T(8,128)} copy(f32[512,512,8]{2,1,0:T(8,128)} %bitcast.13) | data formatting | bytes 16777216 | tf_op jit(solution)/shard_map/jit(_take)/gather | solution.py:110
  964.2 22.9 %while.29 = (s32[]{:T(128)}, bf16[2,512,512]{2,1,0:T(8,128)(2,1)}, f32[2,8,512]{2,1,0:T(8,128)S(1)}, bf16[2,512,512]{1,2,0:T(8,128)(2,1)}, s32[2,512]{1,0:T(2,12...) while((s32[]{:T(128)}, bf16[2,512,512]{2,1,0:T(8,128)(2,1)}, ...), condition=%wide.region_4.5_spmd, body=%wide.region_1.0_spmd.sunk | while | flops 554168320 | bytes 41556588 | solution.py:144
  965.7 5.0 fusion.126
  977.1 5.0 fusion.126
  992.1 3.4 fusion.8
  999.4 45.4 %all_gather.3 = f32[256,512]{1,0:T(8,128)S(1)} all-gather(f32[16,512]{1,0:T(8,128)S(1)} %broadcast_select_fusion), channel_id=1, replica_groups=mesh['tower'=2,'rows'=16] {'rows'}, dimensions={0}, use_global_device_ids=true | all-gather | bytes 557056 | tf_op jit(solution)/shard_map/all_gather | solution.py:180
  1050.2 70.9 %reduce-scatter.2.cloned.1.call-done = f32[16,512]{1,0:T(8,128)} async-done(((f32[256,512]{1,0:T(8,128)}), f32[16,512]{1,0:T(8,128)}) %reduce-scatter.2.cloned.1.call-update) | async-done | bytes 32784 | tf_op jit(solution)/shard_map/reduce_scatter | solution.py:208
  1125.4 4.7 select_convert_fusion
  1130.2 4.5 fusion.56
  1137.8 4.6 fusion.44
  1150.7 74.2 %while.30 = (s32[]{:T(128)}, f32[8,512,512]{1,2,0:T(8,128)}, bf16[2,512,512]{2,1,0:T(8,128)(2,1)}, bf16[2,512,512]{2,1,0:T(8,128)(2,1)}, bf16[2,512,512]{2,1,0:T...) while((s32[]{:T(128)}, f32[8,512,512]{1,2,0:T(8,128)}, ...), condition=%wide.region_15.16_spmd.clone, body=%wide.region_13.15_spmd.clone.sunk | while | flops 1368387584 | bytes 197745472 | solution.py:279
  1153.4 3.4 constant_dynamic-slice_fusion.22
  1159.0 5.0 multiply_reduce_fusion.7
  1164.0 9.8 select_add_fusion.2
  1175.9 4.8 fusion.140
  1188.9 3.4 constant_dynamic-slice_fusion.22
  1194.5 5.0 multiply_reduce_fusion.7
  1199.5 13.0 select_add_fusion.2
  1214.6 4.8 fusion.140
  1225.0 3.4 fusion.53
  1238.3 64.2 %rev.6 = f32[8,512,512]{1,2,0:T(8,128)} reverse(f32[8,512,512]{1,2,0:T(8,128)} %get-tuple-element.126), dimensions={2} | reverse | bytes 16777216 | tf_op jit(solution)/shard_map/rev | solution.py:81
  1302.6 9.6 copy.71
  1312.2 11.6 pad_bitcast_fusion
  1323.9 15.4 %copy.73 = f32[1,8,512,1024]{3,1,2,0:T(8,128)S(1)} copy(f32[1,8,512,1024]{3,2,1,0:T(8,128)} %pad_bitcast_fusion) | data formatting | bytes 33554432
  1339.3 6.0 slice.14
  1345.3 13.0 reshape.408
  1358.2 17.5 %reshape.392 = f32[8,512,1023]{2,1,0:T(8,128)} reshape(f32[4190208]{0:T(1024)} %reshape.408) | data formatting | bytes 33521664 | tf_op jit(solution)/shard_map/reshape | solution.py:84
  1375.8 7.4 reduce_sum.180
  1389.2 37.9 %all-reduce.1 = (f32[512]{0:T(512)}, f32[32,8]{0,1:T(8,128)}, f32[512]{0:T(512)}, f32[1]{0:T(128)}, f32[4]{0:T(128)S(1)}) all-reduce(f32[512]{0:T(512)S(1)} %get-tuple-element.208, f32[32,8]{0,1:T(8,128)S(1)} %fusion.48, f32[512]{0:T(512)S(1)} %copy-done.46, f32[1]{0:T(128)} %bitcast.27, ...), channel_id=1, replica_groups=mesh['tower'=2,'rows'=16] {'tower','rows'}, use_global_device_ids=true, to_apply=%region_18.19 | all-reduce | flops 1285 | bytes 10280 | tf_op jit(solution)/shard_map/psum | solution.py:302
  1429.5 4.1 fusion.18
  1433.6 32.4 %all-reduce.5.cloned.1.call-done = (f32[512,512]{1,0:T(8,128)}, f32[512,512]{1,0:T(8,128)}, f32[512,512]{1,0:T(8,128)}, f32[512,512]{1,0:T(8,128)}, f32[512,2048]{1,0:T(8,128)}, /*index=5*/f32[2048,512]{1,0:T(8,128)}) async-done(((f32[512,512]{1,0:T(8,128)}, f32[512,512]{1,0:T(8,128)}, f32[512,512]{1,0:T(8,128)}, f32[512,512]{1,0:T(8,128)}, f32[512,2048]{1,0:T(8,128)}, /*index=5*/f32[2048,512]{1,0:T(8,128)}), ...) | async-done | bytes 12582928 | tf_op jit(solution)/shard_map/psum | solution.py:302
  (235 shorter events, 117.2 us)
Async XLA Ops:
  7.2 982.5 %copy-start = (bf16[512,2048]{1,0:T(8,128)(2,1)S(1)}, bf16[512,2048]{1,0:T(8,128)(2,1)}, u32[]{:S(2)}) copy-start(bf16[512,2048]{1,0:T(8,128)(2,1)} %param.28) | copy-start | bytes 6291460
  7.2 1114.0 %reduce-scatter.2.cloned.1.call-start = ((), (), s32[]{:S(2)}) async-start(), calls=%async_computation.1 | async-start | bytes 557056 | tf_op jit(solution)/shard_map/reduce_scatter | solution.py:208
  7.2 3.8 copy-start.29
  22.7 3.7 copy-start.44
  892.2 70.9 %copy-start.32 = (s32[1,2,512]{2,1,0:T(2,128)S(1)}, s32[1,2,512]{2,1,0:T(2,128)}, u32[]{:S(2)}) copy-start(s32[1,2,512]{2,1,0:T(2,128)} %param.19) | copy-start | bytes 12292
  992.1 3.5 copy-start.50
  996.9 124.2 %copy-start.5 = (bf16[1,2,512,512]{3,2,1,0:T(8,128)(2,1)S(1)}, bf16[1,2,512,512]{3,2,1,0:T(8,128)(2,1)}, u32[]{:S(2)}) copy-start(bf16[1,2,512,512]{3,2,1,0:T(8,128)(2,1)} %param.18) | copy-start | bytes 3145732
  996.9 124.2 %copy-start.35 = (f32[512]{0:T(512)S(1)}, f32[512]{0:T(512)}, u32[]{:S(2)}) copy-start(f32[512]{0:T(512)} %param.21) | copy-start | bytes 6148
  996.9 124.2 %copy-start.39 = (f32[2,512]{1,0:T(2,128)S(1)}, f32[2,512]{1,0:T(2,128)}, u32[]{:S(2)}) copy-start(f32[2,512]{1,0:T(2,128)} %get-tuple-element.281) | copy-start | bytes 12292
  998.0 1.3 collective-permute-start
  1046.2 4.0 copy-start.40
  1048.5 417.5 %all-reduce.5.cloned.1.call-start = ((), (), s32[]{:S(2)}) async-start(), calls=%async_computation.2 | async-start | bytes 25165824 | tf_op jit(solution)/shard_map/psum | solution.py:302
  1050.2 72.2 %collective-permute-start.1 = (f32[8,512]{1,0:T(8,128)S(1)}, f32[8,512]{1,0:T(8,128)S(1)}, u32[]{:S(2)}, u32[]{:S(2)}) collective-permute-start(f32[8,512]{1,0:T(8,128)S(1)} %convolution_multiply_fusion.1), channel_id=1, source_target_pairs={{0,16},{16,0},{1,17},{17,1},{2,18},{18,2},{3,19},{19,3},{4,20},{20... | collective-permute-start | bytes 49160 | tf_op jit(solution)/shard_map/ppermute | solution.py:19
  1121.2 1.4 collective-permute-start.2
  1125.4 4.7 copy-start.51
  1130.1 4.5 copy-start.9
  1143.4 3.8 copy-start.7
  1152.0 6.9 copy-start.3
  1153.4 10.6 copy-start.2
  1187.6 6.9 copy-start.3
  1188.9 10.6 copy-start.2
  1224.9 3.4 copy-start.17
  1224.9 3.4 copy-start.23
  1233.4 4.4 copy-start.41
  1233.4 4.4 copy-start.43
  1233.4 4.4 copy-start.45
  1375.8 8.0 copy-start.31
  1375.8 8.4 copy-start.16
  1375.8 8.4 copy-start.27
  1466.1 3.4 copy-start.25
  1466.1 4.4 copy-start.24
  1471.6 3.7 copy-start.20
  (30 other events, 60.8 us)
Sparse Core Ops, SparseCore 0:
  1048.7 72.4 reduce-scatter.1
  1231.9 234.1 all-reduce.4
where the time goes:
time: 1500 us; the launch traced here: 1490 us
  local copies, waits for them, and re-layouts  1130 us (75%)
  waiting for transfers between devices  104 us (7%)
  matrix products  95.6 us (6%)
  blocking collectives  83.3 us (6%)
  other arithmetic  51.3 us (3%)
  between operations  17.1 us (1%)
    gather x2, local copies, waits for them, and re-layouts, shards(): jnp.take(position_table.T, jnp.asarray(bucket_index), axis=1)  937 us
    reduce_scatter x1, waiting for transfers between devices, shards(): lax.psum_scatter(lax.dot_general(similarity_gradient, my_queries, (((0,),...  70.9 us
    unnamed x108, local copies, waits for them, and re-layouts  70.5 us
    rev x1, local copies, waits for them, and re-layouts, diagonal_sums(): flipped = square[:, :, ::-1]  64.2 us
    all_gather x1, blocking collectives, shards(): lax.all_gather(document_vectors, 'rows', axis=0, tiled=True)  45.4 us
    psum x1, blocking collectives, shards(): lax.psum((attention_gain_grad, query_grad, key_grad, value_grad, output_g...  37.9 us
    psum x1, waiting for transfers between devices, shards(): lax.psum((attention_gain_grad, query_grad, key_grad, value_grad, output_g...  32.4 us
  transfers between devices with their start and end apart: 5, of which 4 were waited for; matrix products, arithmetic and copies ran while one was open for 11% of the time, Pallas kernels for 0%

commit v1 on v0

--- a/solution.py
+++ b/solution.py
@@ -177,7 +177,12 @@
     partner = from_partner(embedded_tokens, "tower", 0)
     query_vectors = jnp.where(is_query, embedded_tokens, partner)
     document_vectors = jnp.where(is_query, partner, embedded_tokens)
-    gathered_documents = lax.all_gather(document_vectors, "rows", axis=0, tiled=True)
+    ring = [document_vectors]
+    for hop in range(15):
+        ring.append(lax.ppermute(ring[-1], "rows", [(dev, (dev + 1) % 16) for dev in range(16)]))
+    gathered_documents = jnp.roll(
+        jnp.concatenate(ring[::-1], axis=0), (lax.axis_index("rows") + 1) * ring[0].shape[0], axis=0
+    )
     item_total = gathered_documents.shape[0]
     half_items = items_here // 2
     my_queries = lax.dynamic_slice_in_dim(query_vectors, tower_index * half_items, half_items, 0)

time: 1500 us -> 1580 us (1.053)
  waiting for transfers between devices: 104 us -> 215 us
  blocking collectives: 83.3 us -> 37.9 us
    ppermute x0 -> x15, waiting for transfers between devices: none -> 111 us  [shards(): lax.ppermute(ring[-1], 'rows', [(dev, (dev + 1) % 16) for dev in range(16)])]
    all_gather x1 -> x0, blocking collectives: 45.4 us -> none  [shards(): lax.all_gather(document_vectors, 'rows', axis=0, tiled=True)]
    unnamed x108 -> x167, local copies, waits for them, and re-layouts: 70.5 us -> 81.7 us
  transfers between devices with their start and end apart: 5 -> 20, of which waited for: 4 -> 18; matrix products, arithmetic and copies ran while one was open for 11% -> 10% of each run, Pallas kernels for 0% -> 0%
where the time goes in v1:
time: 1580 us; the launch traced here: 1560 us
  local copies, waits for them, and re-layouts  1140 us (72%)
  waiting for transfers between devices  215 us (14%)
  matrix products  95.6 us (6%)
  other arithmetic  52.1 us (3%)
  blocking collectives  37.9 us (2%)
  between operations  17.3 us (1%)
    gather x2, local copies, waits for them, and re-layouts, shards(): jnp.take(position_table.T, jnp.asarray(bucket_index), axis=1)  932 us
    ppermute x15, waiting for transfers between devices, shards(): lax.ppermute(ring[-1], 'rows', [(dev, (dev + 1) % 16) for dev in range(16)])  111 us
    unnamed x167, local copies, waits for them, and re-layouts  81.7 us
    reduce_scatter x1, waiting for transfers between devices, shards(): lax.psum_scatter(lax.dot_general(similarity_gradient, my_queries, (((0,),...  70.9 us
    rev x1, local copies, waits for them, and re-layouts, diagonal_sums(): flipped = square[:, :, ::-1]  64.3 us
    psum x1, blocking collectives, shards(): lax.psum((attention_gain_grad, query_grad, key_grad, value_grad, output_g...  37.9 us
    psum x1, waiting for transfers between devices, shards(): lax.psum((attention_gain_grad, query_grad, key_grad, value_grad, output_g...  32 us
  transfers between devices with their start and end apart: 20, of which 18 were waited for; matrix products, arithmetic and copies ran while one was open for 10% of the time, Pallas kernels for 0%

profile of v1, /device:TPU:0, one launch (start us, length us, event | category | flops | bytes accessed | tf_op | source)
XLA Modules:
  0.0 1562.8 jit_solution(18256201222627054624)
XLA Ops:
  26.5 861.5 %gather_fusion = f32[262144,8]{1,0:T(8,128)} fusion(f32[8,32]{0,1:T(8,128)S(1)} %bitcast.201, s32[262144]{0:T(1024)S(1)} %broadcast_clamp_fusion), kind=kCustom, calls=%fused_computation | custom fusion | bytes 17825792 | tf_op jit(solution)/shard_map/jit(_take)/gather | solution.py:110
  888.0 70.9 %copy.45 = f32[512,512,8]{0,1,2:T(8,128)} copy(f32[512,512,8]{2,1,0:T(8,128)} %bitcast.13) | data formatting | bytes 16777216 | tf_op jit(solution)/shard_map/jit(_take)/gather | solution.py:110
  960.0 22.9 %while.29 = (s32[]{:T(128)}, bf16[2,512,512]{2,1,0:T(8,128)(2,1)}, f32[2,8,512]{2,1,0:T(8,128)S(1)}, bf16[2,512,512]{1,2,0:T(8,128)(2,1)}, s32[2,512]{1,0:T(2,12...) while((s32[]{:T(128)}, bf16[2,512,512]{2,1,0:T(8,128)(2,1)}, ...), condition=%wide.region_4.5_spmd, body=%wide.region_1.0_spmd.sunk | while | flops 554168320 | bytes 41556588 | solution.py:144
  998.0 5.9 collective-permute-done.1
  1003.9 7.5 collective-permute-done.2
  1011.4 7.5 collective-permute-done.3
  1018.9 7.5 collective-permute-done.4
  1026.4 7.5 collective-permute-done.5
  1034.0 7.8 collective-permute-done.6
  1041.7 7.5 collective-permute-done.7
  1049.2 7.5 collective-permute-done.8
  1056.8 7.5 collective-permute-done.9
  1064.3 7.5 collective-permute-done.10
  1072.4 7.5 collective-permute-done.11
  1080.5 7.5 collective-permute-done.12
  1088.6 7.5 collective-permute-done.13
  1096.7 7.5 collective-permute-done.14
  1104.4 7.4 collective-permute-done.15
  1125.9 70.9 %reduce-scatter.2.cloned.1.call-done = f32[16,512]{1,0:T(8,128)} async-done(((f32[256,512]{1,0:T(8,128)}), f32[16,512]{1,0:T(8,128)}) %reduce-scatter.2.cloned.1.call-update) | async-done | bytes 32784 | tf_op jit(solution)/shard_map/reduce_scatter | solution.py:213
  1226.9 74.4 %while.30 = (s32[]{:T(128)}, f32[8,512,512]{1,2,0:T(8,128)}, bf16[2,512,512]{2,1,0:T(8,128)(2,1)}, bf16[2,512,512]{2,1,0:T(8,128)(2,1)}, bf16[2,512,512]{2,1,0:T...) while((s32[]{:T(128)}, f32[8,512,512]{1,2,0:T(8,128)}, ...), condition=%wide.region_15.16_spmd.clone, body=%wide.region_13.15_spmd.clone.sunk | while | flops 1368387584 | bytes 197745472 | solution.py:284
  1240.1 9.8 select_add_fusion.2
  1275.7 13.0 select_add_fusion.2
  1314.7 64.3 %rev.6 = f32[8,512,512]{1,2,0:T(8,128)} reverse(f32[8,512,512]{1,2,0:T(8,128)} %get-tuple-element.126), dimensions={2} | reverse | bytes 16777216 | tf_op jit(solution)/shard_map/rev | solution.py:81
  1379.1 9.6 copy.71
  1388.7 11.6 pad_bitcast_fusion
  1400.3 15.4 copy.73
  1415.7 6.1 slice.14
  1421.8 13.0 reshape.408
  1434.8 17.6 %reshape.392 = f32[8,512,1023]{2,1,0:T(8,128)} reshape(f32[4190208]{0:T(1024)} %reshape.408) | data formatting | bytes 33521664 | tf_op jit(solution)/shard_map/reshape | solution.py:84
  1452.4 7.4 reduce_sum.180
  1465.8 37.9 %all-reduce.1 = (f32[512]{0:T(512)}, f32[32,8]{0,1:T(8,128)}, f32[512]{0:T(512)}, f32[1]{0:T(128)}, f32[4]{0:T(128)S(1)}) all-reduce(f32[512]{0:T(512)S(1)} %get-tuple-element.208, f32[32,8]{0,1:T(8,128)S(1)} %fusion.51, f32[512]{0:T(512)S(1)} %copy-done.60, f32[1]{0:T(128)} %bitcast.27, ...), channel_id=1, replica_groups=mesh['tower'=2,'rows'=16] {'tower','rows'}, use_global_device_ids=true, to_apply=%region_18.19 | all-reduce | flops 1285 | bytes 10280 | tf_op jit(solution)/shard_map/psum | solution.py:307
  1510.3 32.0 %all-reduce.5.cloned.1.call-done = (f32[512,512]{1,0:T(8,128)}, f32[512,512]{1,0:T(8,128)}, f32[512,512]{1,0:T(8,128)}, f32[512,512]{1,0:T(8,128)}, f32[512,2048]{1,0:T(8,128)}, /*index=5*/f32[2048,512]{1,0:T(8,128)}) async-done(((f32[512,512]{1,0:T(8,128)}, f32[512,512]{1,0:T(8,128)}, f32[512,512]{1,0:T(8,128)}, f32[512,512]{1,0:T(8,128)}, f32[512,2048]{1,0:T(8,128)}, /*index=5*/f32[2048,512]{1,0:T(8,128)}), ...) | async-done | bytes 12582928 | tf_op jit(solution)/shard_map/psum | solution.py:307
  (324 shorter events, 192.7 us)
Async XLA Ops:
  7.2 978.3 %copy-start = (bf16[512,2048]{1,0:T(8,128)(2,1)S(1)}, bf16[512,2048]{1,0:T(8,128)(2,1)}, u32[]{:S(2)}) copy-start(bf16[512,2048]{1,0:T(8,128)(2,1)} %param.28) | copy-start | bytes 6291460
  7.2 1189.6 %reduce-scatter.2.cloned.1.call-start = ((), (), s32[]{:S(2)}) async-start(), calls=%async_computation.1 | async-start | bytes 557056 | tf_op jit(solution)/shard_map/reduce_scatter | solution.py:213
  888.0 70.9 %copy-start.32 = (s32[1,2,512]{2,1,0:T(2,128)S(1)}, s32[1,2,512]{2,1,0:T(2,128)}, u32[]{:S(2)}) copy-start(s32[1,2,512]{2,1,0:T(2,128)} %param.19) | copy-start | bytes 12292
  959.0 32.4 %copy-start.53 = (f32[2,8]{1,0:T(2,128)}, f32[2,8]{1,0:T(2,128)S(1)}, u32[]{:S(2)}) copy-start(f32[2,8]{1,0:T(2,128)S(1)} %convert_reduce_fusion) | copy-start | bytes 196
  991.4 112.9 %copy-start.63 = (s32[16]{0:T(128)S(1)}, s32[16]{0:T(128)}, u32[]{:S(2)}) copy-start(s32[16]{0:T(128)} %param.20) | copy-start | bytes 196
  993.8 1.3 collective-permute-start
  995.1 93.5 %copy-start.39 = (f32[16,512]{1,0:T(8,128)}, f32[16,512]{1,0:T(8,128)S(1)}, u32[]{:S(2)}) copy-start(f32[16,512]{1,0:T(8,128)S(1)} %collective-permute-done) | copy-start | bytes 98308
  995.2 8.7 collective-permute-start.1
  1003.9 7.5 collective-permute-start.2
  1011.4 7.5 collective-permute-start.3
  1018.9 7.5 collective-permute-start.4
  1026.4 7.5 collective-permute-start.5
  1034.0 7.8 collective-permute-start.6
  1041.7 7.5 collective-permute-start.7
  1049.2 7.5 collective-permute-start.8
  1056.8 7.5 collective-permute-start.9
  1064.3 7.5 collective-permute-start.10
  1072.4 7.5 collective-permute-start.11
  1080.5 7.5 collective-permute-start.12
  1088.6 7.5 collective-permute-start.13
  1096.7 7.5 collective-permute-start.14
  1104.2 7.5 collective-permute-start.15
  1104.4 18.3 %copy-start.57 = (s32[8]{0:T(128)}, s32[8]{0:T(128)S(1)}, u32[]{:S(2)}) copy-start(s32[8]{0:T(128)S(1)} %dynamic_slice.45) | copy-start | bytes 100
  1112.4 84.4 %copy-start.5 = (bf16[1,2,512,512]{3,2,1,0:T(8,128)(2,1)S(1)}, bf16[1,2,512,512]{3,2,1,0:T(8,128)(2,1)}, u32[]{:S(2)}) copy-start(bf16[1,2,512,512]{3,2,1,0:T(8,128)(2,1)} %param.18) | copy-start | bytes 3145732
  1112.4 84.4 %copy-start.45 = (f32[512]{0:T(512)S(1)}, f32[512]{0:T(512)}, u32[]{:S(2)}) copy-start(f32[512]{0:T(512)} %param.21) | copy-start | bytes 6148
  1121.3 77.5 %copy-start.50 = (f32[16]{0:T(128)S(1)}, f32[16]{0:T(128)}, u32[]{:S(2)}) copy-start(f32[16]{0:T(128)} %copy-done.49) | copy-start | bytes 196
  1121.9 76.8 %copy-start.51 = (f32[8]{0:T(128)}, f32[8]{0:T(128)S(1)}, u32[]{:S(2)}) copy-start(f32[8]{0:T(128)S(1)} %get-tuple-element.286) | copy-start | bytes 100
  1121.9 77.1 %copy-start.54 = (f32[2,8]{1,0:T(2,128)S(1)}, f32[2,8]{1,0:T(2,128)}, u32[]{:S(2)}) copy-start(f32[2,8]{1,0:T(2,128)} %copy-done.53) | copy-start | bytes 196
  1122.7 76.1 %copy-start.55 = (f32[8]{0:T(128)}, f32[8]{0:T(128)S(1)}, u32[]{:S(2)}) copy-start(f32[8]{0:T(128)S(1)} %get-tuple-element.211) | copy-start | bytes 100
  1124.2 418.1 %all-reduce.5.cloned.1.call-start = ((), (), s32[]{:S(2)}) async-start(), calls=%async_computation.2 | async-start | bytes 25165824 | tf_op jit(solution)/shard_map/psum | solution.py:307
  1125.9 72.9 %collective-permute-start.16 = (f32[8,512]{1,0:T(8,128)S(1)}, f32[8,512]{1,0:T(8,128)S(1)}, u32[]{:S(2)}, u32[]{:S(2)}) collective-permute-start(f32[8,512]{1,0:T(8,128)S(1)} %convolution_multiply_fusion.1), channel_id=1, source_target_pairs={{0,16},{16,0},{1,17},{17,1},{2,18},{18,2},{3,19},{19,3},{4,20},{20... | collective-permute-start | bytes 49160 | tf_op jit(solution)/shard_map/ppermute | solution.py:19
  1196.8 2.0 collective-permute-start.17
  (59 other events, 217.2 us)
Sparse Core Ops, SparseCore 0:
  1124.3 72.4 reduce-scatter.1
  1308.3 233.9 all-reduce.4
